TPU v7x, 32 devices: a whole 2x2x4 slice. The times are simulated.
32 devices in a mesh: event: 2 (over y), dom: 4 (over z), sub: 2 (over x), lane: 2 (over core).
Axes of the slice: x: 2, y: 2, z: 4, core: 2. Of those that a mesh axis runs over, the one named last changes fastest.
Arguments:
- displacement: float32 [3, 65536], P(None, ('event', 'dom', 'sub', 'lane')), parts along dimension 1, may hold values from -6 to 6
- previous: float32 [3, 65536], P(None, ('event', 'dom', 'sub', 'lane')), parts along dimension 1, may hold values from -6 to 6
- traffic_load: float32 [2, 3, 65536], P(None, None, ('event', 'dom', 'sub', 'lane')), parts along dimension 2, may hold values from -6 to 6
- lumped_mass: float32 [32768], P(('dom', 'sub', 'lane')), may hold values from 1 to 4
- stiffness: float32 [32768], P(('dom', 'sub', 'lane')), may hold values from 0.2 to 2
- base_matrix: float32 [24, 24], replicated, as said below
- connectivity: int32 [8, 32768], P(None, ('dom', 'sub', 'lane')), may hold values from 0 to 6143, as said below
- live_elements: int32 [16], P(('dom', 'sub', 'lane')), may hold values from 512 to 2048, as said below
- sensor_nodes: int32 [2048], P(('dom', 'sub', 'lane')), may hold values from 0 to 2047
- sensor_weights: float32 [3, 4096], P(None, ('event', 'dom', 'sub', 'lane')), parts along dimension 1, may hold values from -6 to 6
Outputs:
- sensitivity: float32 [65536], P(('event', 'dom', 'sub', 'lane')), parts along dimension 0
- adjoint_start: float32 [3, 65536], P(None, ('event', 'dom', 'sub', 'lane')), parts along dimension 1
- sensor_response: float32 [3, 4096], P(None, ('event', 'dom', 'sub', 'lane')), parts along dimension 1
There are 2 independent parts, one for each index of `event`. A program takes and returns all parts, laid end to end along the dimension named above; an argument that names none is the same for every part. Nothing has to cross between parts.
Inputs may be any that keep to these rules, and one draw needn't show every extreme that they name: `connectivity`: each slot's eight indices are b, b+1, b+4, b+5, b+2048, b+2048 + 1, b+2048 + 4, b+2048 + 5 for some b; window index w means node w of the node blocks of the device before, the device itself and the device after, laid end to end. `live_elements`: device 0 of every draw has all slots live. `base_matrix`: Symmetric.
All inputs are finite; a program needn't handle non-finite values.
Results may differ from a plain program's by a relative error of at most 0.00015.
Values sent between devices are 32-bit elements; how exact they have to be, the bound alone decides.
A program may use at most 64 MiB of HBM per device.

v0:
```python
import jax
import jax.numpy as jnp
from jax import lax
from jax.sharding import PartitionSpec as P


def passed_along(block, axis, distance):
    devices = range(lax.axis_size(axis))
    route = [(i - distance, i) for i in devices if i - distance in devices]
    return lax.ppermute(block, axis, route)


def extended(block, sides, width):
    for axis, dim in sides:
        count = lax.axis_size(axis)
        forward = [(i, i + 1) for i in range(count - 1)]
        backward = [(target, source) for source, target in forward]
        low = lax.ppermute(
            lax.slice_in_dim(block, block.shape[dim] - width, None, axis=dim), axis, forward
        )
        high = lax.ppermute(lax.slice_in_dim(block, 0, width, axis=dim), axis, backward)
        block = jnp.concatenate([low, block, high], axis=dim)
    return block


def split_sizes(count):
    low = min(128, count)
    high = -(-count // low)
    return (low, high)


def one_hots(index, low, high):
    width = index.shape[0]
    low_hot = (lax.broadcasted_iota(jnp.int32, (low, width), 0) == (index % low)[None, :]).astype(
        jnp.float32
    )
    high_hot = (
        lax.broadcasted_iota(jnp.int32, (high, width), 0) == (index // low)[None, :]
    ).astype(jnp.float32)
    return (low_hot, high_hot)


def pick_columns(table, index, low, high):
    rows = table.shape[0]
    grid = table.reshape(rows, high, low)
    low_hot, high_hot = one_hots(index, low, high)
    partial_rows = jnp.einsum("rhl,le->rhe", grid, low_hot, precision=lax.Precision.HIGHEST)
    return jnp.sum(partial_rows * high_hot[None, :, :], axis=1)


def place_columns(values, index, low, high):
    rows = values.shape[0]
    low_hot, high_hot = one_hots(index, low, high)
    weighted = values[:, None, :] * high_hot[None, :, :]
    placed = jnp.einsum("rhe,le->rhl", weighted, low_hot, precision=lax.Precision.HIGHEST)
    return placed.reshape(rows, high * low)


def window_of(field):
    before = passed_along(field, ("dom", "sub", "lane"), 1)
    after = passed_along(field, ("dom", "sub", "lane"), -1)
    return jnp.concatenate([before, field, after], axis=1)


def reduce_window(forces, node_count):
    middle = forces[:, node_count : 2 * node_count]
    outgoing = jnp.concatenate([forces[:, :node_count], forces[:, 2 * node_count :]], axis=1)
    padded = extended(outgoing, ((("dom", "sub", "lane"), 1),), node_count)
    return middle + padded[:, :node_count] + padded[:, 3 * node_count :]


def assemble(field, corner_blocks, scale, base_matrix):
    node_count = field.shape[1]
    block_count, block_size = corner_blocks.shape
    slot_count = block_count * block_size
    span = 2 * node_count
    offsets = [0, 1, 4, 5, node_count, node_count + 1, node_count + 4, node_count + 5]
    low, high = split_sizes(span)
    window = window_of(field)
    wide = jnp.pad(window, ((0, 0), (0, 8)))
    shifted = jnp.stack([wide[:, start : start + span] for start in offsets], axis=1).reshape(
        24, span
    )

    def gather_block(index):
        return pick_columns(shifted, index, low, high)

    blocked = lax.map(gather_block, corner_blocks)
    local_vals = jnp.transpose(blocked, (1, 0, 2)).reshape(24, slot_count)
    products = jnp.dot(base_matrix, local_vals, precision=lax.Precision.HIGHEST)
    forces = products * scale[None, :]
    force_blocks = jnp.transpose(forces.reshape(24, block_count, block_size), (1, 0, 2))

    def place_block(total, pieces):
        return (total + place_columns(pieces[0], pieces[1], low, high), None)

    corner_forces, unused = lax.scan(
        place_block, jnp.zeros((24, high * low), jnp.float32), (force_blocks, corner_blocks)
    )
    corner_forces = corner_forces.reshape(3, 8, span)
    total_width = 3 * node_count + 8
    spread = jnp.zeros((3, total_width), jnp.float32)
    for which in range(8):
        start = offsets[which]
        spread = spread + jnp.pad(
            corner_forces[:, which], ((0, 0), (start, total_width - start - span))
        )
    return (reduce_window(spread[:, : 3 * node_count], node_count), local_vals, products)


def per_device(
    displacement,
    previous,
    traffic_load,
    lumped_mass,
    stiffness,
    base_matrix,
    connectivity,
    live_elements,
    sensor_nodes,
    sensor_weights,
):
    slot_count = connectivity.shape[1]
    node_count = displacement.shape[1]
    block_size = min(128, slot_count)
    corner_blocks = connectivity[0].reshape(slot_count // block_size, block_size)
    live = (jnp.arange(slot_count) < live_elements[0]).astype(jnp.float32)
    scale = stiffness * live
    force0, vals0, prod0 = assemble(displacement, corner_blocks, scale, base_matrix)
    step_one = 2.0 * displacement - previous + 0.1 * (traffic_load[0] - force0) / lumped_mass
    force1, vals1, prod1 = assemble(step_one, corner_blocks, scale, base_matrix)
    step_two = 2.0 * step_one - displacement + 0.1 * (traffic_load[1] - force1) / lumped_mass
    node_low, node_high = split_sizes(node_count)
    sensor_response = pick_columns(step_two, sensor_nodes, node_low, node_high)
    lam_two = place_columns(sensor_weights, sensor_nodes, node_low, node_high)
    mu_two = 0.1 * lam_two / lumped_mass
    force_mu2, mvals2, mprod2 = assemble(mu_two, corner_blocks, scale, base_matrix)
    lam_one = 2.0 * lam_two - force_mu2
    mu_one = 0.1 * lam_one / lumped_mass
    force_mu1, mvals1, mprod1 = assemble(mu_one, corner_blocks, scale, base_matrix)
    adjoint_start = 2.0 * lam_one - force_mu1 - lam_two
    sensitivity = -live * (jnp.sum(mvals2 * prod1, axis=0) + jnp.sum(mvals1 * prod0, axis=0))
    return (sensitivity, adjoint_start, sensor_response)


def solution(mesh):
    in_specs = (
        P(None, ("event", "dom", "sub", "lane")),
        P(None, ("event", "dom", "sub", "lane")),
        P(None, None, ("event", "dom", "sub", "lane")),
        P(("dom", "sub", "lane")),
        P(("dom", "sub", "lane")),
        P(),
        P(None, ("dom", "sub", "lane")),
        P(("dom", "sub", "lane")),
        P(("dom", "sub", "lane")),
        P(None, ("event", "dom", "sub", "lane")),
    )
    out_specs = (
        P(("event", "dom", "sub", "lane")),
        P(None, ("event", "dom", "sub", "lane")),
        P(None, ("event", "dom", "sub", "lane")),
    )
    return jax.shard_map(
        per_device, mesh=mesh, in_specs=in_specs, out_specs=out_specs, check_vma=False
    )
```

profile of v0, /device:TPU:7, one launch (start us, length us, event | category | flops | bytes accessed | tf_op | source)
XLA Modules:
  0.0 152.7 jit_solution(13818167975632007892)
XLA Ops:
  0.6 0.7 and_select_fusion.17
  1.3 0.7 copy-done.6
  2.2 0.5 copy-done.2
  2.7 3.7 %collective-permute-start = (f32[3,2048]{1,0:T(4,128)S(1)}, f32[3,2048]{1,0:T(4,128)S(1)}, u32[]{:S(2)}, u32[]{:S(2)}) collective-permute-start(f32[3,2048]{1,0:T(4,128)S(1)} %fusion.123), channel_id=1, source_target_pairs={{0,1},{1,2},{2,3},{3,4},{4,5},{5,6},{6,7},{7,8},{8,9},{9,10},{10,1... | collective-permute-start | bytes 73736 | tf_op jit(solution)/shard_map/ppermute | solution.py:10
  6.5 1.9 %collective-permute-start.1 = (f32[3,2048]{1,0:T(4,128)S(1)}, f32[3,2048]{1,0:T(4,128)S(1)}, u32[]{:S(2)}, u32[]{:S(2)}) collective-permute-start(f32[3,2048]{1,0:T(4,128)S(1)} %fusion.123), channel_id=1, source_target_pairs={{1,0},{2,1},{3,2},{4,3},{5,4},{6,5},{7,6},{8,7},{9,8},{10,9},{11,1... | collective-permute-start | bytes 73736 | tf_op jit(solution)/shard_map/ppermute | solution.py:10
  8.4 4.5 %collective-permute-start.2 = (f32[3,2048]{1,0:T(4,128)S(1)}, f32[3,2048]{1,0:T(4,128)S(1)}, u32[]{:S(2)}, u32[]{:S(2)}) collective-permute-start(f32[3,2048]{1,0:T(4,128)S(1)} %copy-done.1), channel_id=1, source_target_pairs={{0,1},{1,2},{2,3},{3,4},{4,5},{5,6},{6,7},{7,8},{8,9},{9,10},{10,1... | collective-permute-start | bytes 73736 | tf_op jit(solution)/shard_map/ppermute | solution.py:10
  13.0 1.9 %collective-permute-start.3 = (f32[3,2048]{1,0:T(4,128)S(1)}, f32[3,2048]{1,0:T(4,128)S(1)}, u32[]{:S(2)}, u32[]{:S(2)}) collective-permute-start(f32[3,2048]{1,0:T(4,128)S(1)} %copy-done.1), channel_id=1, source_target_pairs={{1,0},{2,1},{3,2},{4,3},{5,4},{6,5},{7,6},{8,7},{9,8},{10,9},{11,1... | collective-permute-start | bytes 73736 | tf_op jit(solution)/shard_map/ppermute | solution.py:10
  15.6 0.6 copy-done.5
  17.4 0.7 slice-done
  18.0 7.9 %while.100 = (s32[]{:T(128)}, f32[16,24,128]{2,1,0:T(8,128)S(1)}, s32[16,128]{1,0:T(8,128)S(1)}, f32[3,8,4096]{2,1,0:T(8,128)S(1)}, s32[]{:T(128)}) while((s32[]{:T(128)}, f32[16,24,128]{2,1,0:T(8,128)S(1)}, s32[16,128]{1,0:T(8,128)S(1)}, f32[3,8,4096]{2,1,0:T(8,128)S(1)}, s32[]{:T(128)}) %tuple.304), condition=%wide.region_2.3_spmd, body=%wide.region_0.2_spmd.sunk | while | flops 151216000 | bytes 1253449 | solution.py:88
  26.3 11.7 %while.105 = (s32[]{:T(128)}, f32[24,4096]{1,0:T(8,128)S(1)}, f32[16,24,128]{2,1,0:T(8,128)S(1)}, s32[16,128]{1,0:T(8,128)S(1)}, s32[]{:T(128)}, /*index=5*/s32[]{:T(128)}) while((s32[]{:T(128)}, f32[24,4096]{1,0:T(8,128)S(1)}, f32[16,24,128]{2,1,0:T(8,128)S(1)}, s32[16,128]{1,0:T(8,128)S(1)}, s32[]{:T(128)}, ...), condition=%wide.region_13.14_spmd.clone, body=%wide.region_12.13_spmd.clone.sunk | while | flops 151317376 | bytes 1646683 | solution.py:97
  27.1 0.3 fusion.254
  27.8 0.3 fusion.254
  29.3 0.3 fusion.254
  31.5 0.3 fusion.254
  35.2 0.3 fusion.254
  38.0 0.4 fusion.146
  39.0 4.5 %collective-permute-start.8 = (f32[3,2048]{1,0:T(4,128)S(1)}, f32[3,2048]{1,0:T(4,128)S(1)}, u32[]{:S(2)}, u32[]{:S(2)}) collective-permute-start(f32[3,2048]{1,0:T(4,128)S(1)} %get-tuple-element.663), channel_id=1, source_target_pairs={{0,1},{1,2},{2,3},{3,4},{4,5},{5,6},{6,7},{7,8},{8,9},{9,10},{10,1... | collective-permute-start | bytes 73736 | tf_op jit(solution)/shard_map/ppermute | solution.py:18
  43.5 1.9 %collective-permute-start.9 = (f32[3,2048]{1,0:T(4,128)S(1)}, f32[3,2048]{1,0:T(4,128)S(1)}, u32[]{:S(2)}, u32[]{:S(2)}) collective-permute-start(f32[3,2048]{1,0:T(4,128)S(1)} %get-tuple-element.664), channel_id=1, source_target_pairs={{1,0},{2,1},{3,2},{4,3},{5,4},{6,5},{7,6},{8,7},{9,8},{10,9},{11,1... | collective-permute-start | bytes 73736 | tf_op jit(solution)/shard_map/ppermute | solution.py:21
  46.3 0.7 stack.125
  47.0 2.7 %collective-permute-done.9 = f32[3,2048]{1,0:T(4,128)S(1)} collective-permute-done((f32[3,2048]{1,0:T(4,128)S(1)}, f32[3,2048]{1,0:T(4,128)S(1)}, u32[]{:S(2)}, u32[]{:S(2)}) %collective-permute-start.9) | collective-permute-done | bytes 24608 | tf_op jit(solution)/shard_map/ppermute | solution.py:21
  49.7 1.9 %collective-permute-start.10 = (f32[3,2048]{1,0:T(4,128)S(1)}, f32[3,2048]{1,0:T(4,128)S(1)}, u32[]{:S(2)}, u32[]{:S(2)}) collective-permute-start(f32[3,2048]{1,0:T(4,128)S(1)} %multiply_divide_fusion), channel_id=1, source_target_pairs={{0,1},{1,2},{2,3},{3,4},{4,5},{5,6},{6,7},{7,8},{8,9},{9,10},{10,1... | collective-permute-start | bytes 73736 | tf_op jit(solution)/shard_map/ppermute | solution.py:10
  51.7 7.9 %while.101 = (s32[]{:T(128)}, f32[16,24,128]{2,1,0:T(8,128)S(1)}, s32[16,128]{1,0:T(8,128)S(1)}, f32[3,8,4096]{2,1,0:T(8,128)S(1)}, s32[]{:T(128)}) while((s32[]{:T(128)}, f32[16,24,128]{2,1,0:T(8,128)S(1)}, s32[16,128]{1,0:T(8,128)S(1)}, f32[3,8,4096]{2,1,0:T(8,128)S(1)}, s32[]{:T(128)}) %tuple.298), condition=%wide.region_5.6_spmd, body=%wide.region_3.5_spmd.sunk | while | flops 151216000 | bytes 1253449 | solution.py:88
  59.6 2.4 %collective-permute-start.11 = (f32[3,2048]{1,0:T(4,128)S(1)}, f32[3,2048]{1,0:T(4,128)S(1)}, u32[]{:S(2)}, u32[]{:S(2)}) collective-permute-start(f32[3,2048]{1,0:T(4,128)S(1)} %multiply_divide_fusion), channel_id=1, source_target_pairs={{1,0},{2,1},{3,2},{4,3},{5,4},{6,5},{7,6},{8,7},{9,8},{10,9},{11,1... | collective-permute-start | bytes 73736 | tf_op jit(solution)/shard_map/ppermute | solution.py:10
  62.0 3.7 %collective-permute-done.11 = f32[3,2048]{1,0:T(4,128)S(1)} collective-permute-done((f32[3,2048]{1,0:T(4,128)S(1)}, f32[3,2048]{1,0:T(4,128)S(1)}, u32[]{:S(2)}, u32[]{:S(2)}) %collective-permute-start.11) | collective-permute-done | bytes 24608 | tf_op jit(solution)/shard_map/ppermute | solution.py:10
  66.8 7.9 %while.103 = (s32[]{:T(128)}, f32[16,24,128]{2,1,0:T(8,128)S(1)}, s32[16,128]{1,0:T(8,128)S(1)}, f32[3,8,4096]{2,1,0:T(8,128)S(1)}, s32[]{:T(128)}) while((s32[]{:T(128)}, f32[16,24,128]{2,1,0:T(8,128)S(1)}, s32[16,128]{1,0:T(8,128)S(1)}, f32[3,8,4096]{2,1,0:T(8,128)S(1)}, s32[]{:T(128)}) %tuple.299), condition=%wide.region_16.17_spmd, body=%wide.region_14.16_spmd.sunk | while | flops 151216000 | bytes 1253449 | solution.py:88
  75.4 11.7 %while.104 = (s32[]{:T(128)}, f32[24,4096]{1,0:T(8,128)S(1)}, f32[16,24,128]{2,1,0:T(8,128)S(1)}, s32[16,128]{1,0:T(8,128)S(1)}, s32[]{:T(128)}, /*index=5*/s32[]{:T(128)}) while((s32[]{:T(128)}, f32[24,4096]{1,0:T(8,128)S(1)}, f32[16,24,128]{2,1,0:T(8,128)S(1)}, s32[16,128]{1,0:T(8,128)S(1)}, s32[]{:T(128)}, ...), condition=%wide.region_7.8_spmd.clone, body=%wide.region_6.7_spmd.clone.sunk | while | flops 151317376 | bytes 1646683 | solution.py:97
  76.2 0.3 fusion.248
  76.9 0.3 fusion.248
  80.6 0.3 fusion.248
  87.1 0.4 fusion.147
  88.1 1.9 %collective-permute-start.4 = (f32[3,2048]{1,0:T(4,128)S(1)}, f32[3,2048]{1,0:T(4,128)S(1)}, u32[]{:S(2)}, u32[]{:S(2)}) collective-permute-start(f32[3,2048]{1,0:T(4,128)S(1)} %get-tuple-element.665), channel_id=1, source_target_pairs={{0,1},{1,2},{2,3},{3,4},{4,5},{5,6},{6,7},{7,8},{8,9},{9,10},{10,1... | collective-permute-start | bytes 73736 | tf_op jit(solution)/shard_map/ppermute | solution.py:18
  90.0 2.4 %collective-permute-start.5 = (f32[3,2048]{1,0:T(4,128)S(1)}, f32[3,2048]{1,0:T(4,128)S(1)}, u32[]{:S(2)}, u32[]{:S(2)}) collective-permute-start(f32[3,2048]{1,0:T(4,128)S(1)} %get-tuple-element.666), channel_id=1, source_target_pairs={{1,0},{2,1},{3,2},{4,3},{5,4},{6,5},{7,6},{8,7},{9,8},{10,9},{11,1... | collective-permute-start | bytes 73736 | tf_op jit(solution)/shard_map/ppermute | solution.py:21
  92.5 11.7 %while.106 = (s32[]{:T(128)}, f32[24,4096]{1,0:T(8,128)S(1)}, f32[16,24,128]{2,1,0:T(8,128)S(1)}, s32[16,128]{1,0:T(8,128)S(1)}, s32[]{:T(128)}, /*index=5*/s32[]{:T(128)}) while((s32[]{:T(128)}, f32[24,4096]{1,0:T(8,128)S(1)}, f32[16,24,128]{2,1,0:T(8,128)S(1)}, s32[16,128]{1,0:T(8,128)S(1)}, s32[]{:T(128)}, ...), condition=%wide.region_19.20_spmd.clone, body=%wide.region_18.19_spmd.clone.sunk | while | flops 151317376 | bytes 1646683 | solution.py:97
  105.1 4.1 %collective-permute-start.12 = (f32[3,2048]{1,0:T(4,128)S(1)}, f32[3,2048]{1,0:T(4,128)S(1)}, u32[]{:S(2)}, u32[]{:S(2)}) collective-permute-start(f32[3,2048]{1,0:T(4,128)S(1)} %get-tuple-element.661), channel_id=1, source_target_pairs={{0,1},{1,2},{2,3},{3,4},{4,5},{5,6},{6,7},{7,8},{8,9},{9,10},{10,1... | collective-permute-start | bytes 73736 | tf_op jit(solution)/shard_map/ppermute | solution.py:18
  109.2 1.9 %collective-permute-start.13 = (f32[3,2048]{1,0:T(4,128)S(1)}, f32[3,2048]{1,0:T(4,128)S(1)}, u32[]{:S(2)}, u32[]{:S(2)}) collective-permute-start(f32[3,2048]{1,0:T(4,128)S(1)} %get-tuple-element.662), channel_id=1, source_target_pairs={{1,0},{2,1},{3,2},{4,3},{5,4},{6,5},{7,6},{8,7},{9,8},{10,9},{11,1... | collective-permute-start | bytes 73736 | tf_op jit(solution)/shard_map/ppermute | solution.py:21
  111.2 4.5 %collective-permute-start.6 = (f32[3,2048]{1,0:T(4,128)S(1)}, f32[3,2048]{1,0:T(4,128)S(1)}, u32[]{:S(2)}, u32[]{:S(2)}) collective-permute-start(f32[3,2048]{1,0:T(4,128)S(1)} %divide_add_fusion.1), channel_id=1, source_target_pairs={{0,1},{1,2},{2,3},{3,4},{4,5},{5,6},{6,7},{7,8},{8,9},{9,10},{10,1... | collective-permute-start | bytes 73736 | tf_op jit(solution)/shard_map/ppermute | solution.py:10
  115.7 2.1 %collective-permute-start.7 = (f32[3,2048]{1,0:T(4,128)S(1)}, f32[3,2048]{1,0:T(4,128)S(1)}, u32[]{:S(2)}, u32[]{:S(2)}) collective-permute-start(f32[3,2048]{1,0:T(4,128)S(1)} %divide_add_fusion.1), channel_id=1, source_target_pairs={{1,0},{2,1},{3,2},{4,3},{5,4},{6,5},{7,6},{8,7},{9,8},{10,9},{11,1... | collective-permute-start | bytes 73736 | tf_op jit(solution)/shard_map/ppermute | solution.py:10
  117.9 0.7 bitcast_subtract_fusion
  118.6 3.3 %collective-permute-done.7 = f32[3,2048]{1,0:T(4,128)S(1)} collective-permute-done((f32[3,2048]{1,0:T(4,128)S(1)}, f32[3,2048]{1,0:T(4,128)S(1)}, u32[]{:S(2)}, u32[]{:S(2)}) %collective-permute-start.7) | collective-permute-done | bytes 24608 | tf_op jit(solution)/shard_map/ppermute | solution.py:10
  122.9 7.9 %while.102 = (s32[]{:T(128)}, f32[16,24,128]{2,1,0:T(8,128)S(1)}, s32[16,128]{1,0:T(8,128)S(1)}, f32[3,8,4096]{2,1,0:T(8,128)S(1)}, s32[]{:T(128)}) while((s32[]{:T(128)}, f32[16,24,128]{2,1,0:T(8,128)S(1)}, s32[16,128]{1,0:T(8,128)S(1)}, f32[3,8,4096]{2,1,0:T(8,128)S(1)}, s32[]{:T(128)}) %tuple.302), condition=%wide.region_10.11_spmd, body=%wide.region_8.10_spmd.sunk | while | flops 151216000 | bytes 1253449 | solution.py:88
  131.2 11.7 %while.107 = (s32[]{:T(128)}, f32[24,4096]{1,0:T(8,128)S(1)}, f32[16,24,128]{2,1,0:T(8,128)S(1)}, s32[16,128]{1,0:T(8,128)S(1)}, s32[]{:T(128)}, /*index=5*/s32[]{:T(128)}) while((s32[]{:T(128)}, f32[24,4096]{1,0:T(8,128)S(1)}, f32[16,24,128]{2,1,0:T(8,128)S(1)}, s32[16,128]{1,0:T(8,128)S(1)}, s32[]{:T(128)}, ...), condition=%wide.region_21.22_spmd.clone, body=%wide.region_20.21_spmd.clone.sunk | while | flops 151317376 | bytes 1646683 | solution.py:97
  131.3 0.3 fusion.266
  143.8 1.9 %collective-permute-start.14 = (f32[3,2048]{1,0:T(4,128)S(1)}, f32[3,2048]{1,0:T(4,128)S(1)}, u32[]{:S(2)}, u32[]{:S(2)}) collective-permute-start(f32[3,2048]{1,0:T(4,128)S(1)} %get-tuple-element.659), channel_id=1, source_target_pairs={{0,1},{1,2},{2,3},{3,4},{4,5},{5,6},{6,7},{7,8},{8,9},{9,10},{10,1... | collective-permute-start | bytes 73736 | tf_op jit(solution)/shard_map/ppermute | solution.py:18
  145.8 2.4 %collective-permute-start.15 = (f32[3,2048]{1,0:T(4,128)S(1)}, f32[3,2048]{1,0:T(4,128)S(1)}, u32[]{:S(2)}, u32[]{:S(2)}) collective-permute-start(f32[3,2048]{1,0:T(4,128)S(1)} %get-tuple-element.660), channel_id=1, source_target_pairs={{1,0},{2,1},{3,2},{4,3},{5,4},{6,5},{7,6},{8,7},{9,8},{10,9},{11,1... | collective-permute-start | bytes 73736 | tf_op jit(solution)/shard_map/ppermute | solution.py:21
  148.2 0.6 add_multiply_fusion
  148.8 3.1 %collective-permute-done.15 = f32[3,2048]{1,0:T(4,128)S(1)} collective-permute-done((f32[3,2048]{1,0:T(4,128)S(1)}, f32[3,2048]{1,0:T(4,128)S(1)}, u32[]{:S(2)}, u32[]{:S(2)}) %collective-permute-start.15) | collective-permute-done | bytes 24608 | tf_op jit(solution)/shard_map/ppermute | solution.py:21
  151.9 0.8 fusion.74
  (888 shorter events, 76.9 us)
Async XLA Ops:
  0.6 25.3 %copy-start = (f32[24,24]{1,0:T(8,128)S(1)}, f32[24,24]{1,0:T(8,128)}, u32[]{:S(2)}) copy-start(f32[24,24]{1,0:T(8,128)} %param.31) | copy-start | bytes 6916
  1.3 0.7 copy-start.6
  2.0 0.7 copy-start.2
  2.0 13.5 %copy-start.3 = (f32[2,3,2048]{2,0,1:T(2,128)S(1)}, f32[2,3,2048]{2,0,1:T(2,128)}, u32[]{:S(2)}) copy-start(f32[2,3,2048]{2,0,1:T(2,128)} %param.28) | copy-start | bytes 147460
  2.7 5.7 %copy-start.1 = (f32[3,2048]{1,0:T(4,128)S(1)}, f32[3,2048]{1,0:T(4,128)}, u32[]{:S(2)}) copy-start(f32[3,2048]{1,0:T(4,128)} %param.26) | copy-start | bytes 73732
  2.7 13.5 %collective-permute-start = (f32[3,2048]{1,0:T(4,128)S(1)}, f32[3,2048]{1,0:T(4,128)S(1)}, u32[]{:S(2)}, u32[]{:S(2)}) collective-permute-start(f32[3,2048]{1,0:T(4,128)S(1)} %fusion.123), channel_id=1, source_target_pairs={{0,1},{1,2},{2,3},{3,4},{4,5},{5,6},{6,7},{7,8},{8,9},{9,10},{10,1... | collective-permute-start | bytes 73736 | tf_op jit(solution)/shard_map/ppermute | solution.py:10
  6.5 9.8 %collective-permute-start.1 = (f32[3,2048]{1,0:T(4,128)S(1)}, f32[3,2048]{1,0:T(4,128)S(1)}, u32[]{:S(2)}, u32[]{:S(2)}) collective-permute-start(f32[3,2048]{1,0:T(4,128)S(1)} %fusion.123), channel_id=1, source_target_pairs={{1,0},{2,1},{3,2},{4,3},{5,4},{6,5},{7,6},{8,7},{9,8},{10,9},{11,1... | collective-permute-start | bytes 73736 | tf_op jit(solution)/shard_map/ppermute | solution.py:10
  8.4 37.1 %collective-permute-start.2 = (f32[3,2048]{1,0:T(4,128)S(1)}, f32[3,2048]{1,0:T(4,128)S(1)}, u32[]{:S(2)}, u32[]{:S(2)}) collective-permute-start(f32[3,2048]{1,0:T(4,128)S(1)} %copy-done.1), channel_id=1, source_target_pairs={{0,1},{1,2},{2,3},{3,4},{4,5},{5,6},{6,7},{7,8},{8,9},{9,10},{10,1... | collective-permute-start | bytes 73736 | tf_op jit(solution)/shard_map/ppermute | solution.py:10
  13.0 32.5 %collective-permute-start.3 = (f32[3,2048]{1,0:T(4,128)S(1)}, f32[3,2048]{1,0:T(4,128)S(1)}, u32[]{:S(2)}, u32[]{:S(2)}) collective-permute-start(f32[3,2048]{1,0:T(4,128)S(1)} %copy-done.1), channel_id=1, source_target_pairs={{1,0},{2,1},{3,2},{4,3},{5,4},{6,5},{7,6},{8,7},{9,8},{10,9},{11,1... | collective-permute-start | bytes 73736 | tf_op jit(solution)/shard_map/ppermute | solution.py:10
  15.5 0.7 copy-start.5
  17.3 0.7 slice-start
  39.0 8.0 %collective-permute-start.8 = (f32[3,2048]{1,0:T(4,128)S(1)}, f32[3,2048]{1,0:T(4,128)S(1)}, u32[]{:S(2)}, u32[]{:S(2)}) collective-permute-start(f32[3,2048]{1,0:T(4,128)S(1)} %get-tuple-element.663), channel_id=1, source_target_pairs={{0,1},{1,2},{2,3},{3,4},{4,5},{5,6},{6,7},{7,8},{8,9},{9,10},{10,1... | collective-permute-start | bytes 73736 | tf_op jit(solution)/shard_map/ppermute | solution.py:18
  43.5 6.1 %collective-permute-start.9 = (f32[3,2048]{1,0:T(4,128)S(1)}, f32[3,2048]{1,0:T(4,128)S(1)}, u32[]{:S(2)}, u32[]{:S(2)}) collective-permute-start(f32[3,2048]{1,0:T(4,128)S(1)} %get-tuple-element.664), channel_id=1, source_target_pairs={{1,0},{2,1},{3,2},{4,3},{5,4},{6,5},{7,6},{8,7},{9,8},{10,9},{11,1... | collective-permute-start | bytes 73736 | tf_op jit(solution)/shard_map/ppermute | solution.py:21
  49.7 12.3 %collective-permute-start.10 = (f32[3,2048]{1,0:T(4,128)S(1)}, f32[3,2048]{1,0:T(4,128)S(1)}, u32[]{:S(2)}, u32[]{:S(2)}) collective-permute-start(f32[3,2048]{1,0:T(4,128)S(1)} %multiply_divide_fusion), channel_id=1, source_target_pairs={{0,1},{1,2},{2,3},{3,4},{4,5},{5,6},{6,7},{7,8},{8,9},{9,10},{10,1... | collective-permute-start | bytes 73736 | tf_op jit(solution)/shard_map/ppermute | solution.py:10
  59.6 6.1 %collective-permute-start.11 = (f32[3,2048]{1,0:T(4,128)S(1)}, f32[3,2048]{1,0:T(4,128)S(1)}, u32[]{:S(2)}, u32[]{:S(2)}) collective-permute-start(f32[3,2048]{1,0:T(4,128)S(1)} %multiply_divide_fusion), channel_id=1, source_target_pairs={{1,0},{2,1},{3,2},{4,3},{5,4},{6,5},{7,6},{8,7},{9,8},{10,9},{11,1... | collective-permute-start | bytes 73736 | tf_op jit(solution)/shard_map/ppermute | solution.py:10
  88.1 23.0 %collective-permute-start.4 = (f32[3,2048]{1,0:T(4,128)S(1)}, f32[3,2048]{1,0:T(4,128)S(1)}, u32[]{:S(2)}, u32[]{:S(2)}) collective-permute-start(f32[3,2048]{1,0:T(4,128)S(1)} %get-tuple-element.665), channel_id=1, source_target_pairs={{0,1},{1,2},{2,3},{3,4},{4,5},{5,6},{6,7},{7,8},{8,9},{9,10},{10,1... | collective-permute-start | bytes 73736 | tf_op jit(solution)/shard_map/ppermute | solution.py:18
  90.0 21.1 %collective-permute-start.5 = (f32[3,2048]{1,0:T(4,128)S(1)}, f32[3,2048]{1,0:T(4,128)S(1)}, u32[]{:S(2)}, u32[]{:S(2)}) collective-permute-start(f32[3,2048]{1,0:T(4,128)S(1)} %get-tuple-element.666), channel_id=1, source_target_pairs={{1,0},{2,1},{3,2},{4,3},{5,4},{6,5},{7,6},{8,7},{9,8},{10,9},{11,1... | collective-permute-start | bytes 73736 | tf_op jit(solution)/shard_map/ppermute | solution.py:21
  105.1 6.0 %copy-start.4 = (f32[3,2048]{1,0:T(4,128)S(1)}, f32[3,2048]{1,0:T(4,128)}, u32[]{:S(2)}) copy-start(f32[3,2048]{1,0:T(4,128)} %param.27) | copy-start | bytes 73732
  105.1 12.7 %collective-permute-start.12 = (f32[3,2048]{1,0:T(4,128)S(1)}, f32[3,2048]{1,0:T(4,128)S(1)}, u32[]{:S(2)}, u32[]{:S(2)}) collective-permute-start(f32[3,2048]{1,0:T(4,128)S(1)} %get-tuple-element.661), channel_id=1, source_target_pairs={{0,1},{1,2},{2,3},{3,4},{4,5},{5,6},{6,7},{7,8},{8,9},{9,10},{10,1... | collective-permute-start | bytes 73736 | tf_op jit(solution)/shard_map/ppermute | solution.py:18
  109.2 8.7 %collective-permute-start.13 = (f32[3,2048]{1,0:T(4,128)S(1)}, f32[3,2048]{1,0:T(4,128)S(1)}, u32[]{:S(2)}, u32[]{:S(2)}) collective-permute-start(f32[3,2048]{1,0:T(4,128)S(1)} %get-tuple-element.662), channel_id=1, source_target_pairs={{1,0},{2,1},{3,2},{4,3},{5,4},{6,5},{7,6},{8,7},{9,8},{10,9},{11,1... | collective-permute-start | bytes 73736 | tf_op jit(solution)/shard_map/ppermute | solution.py:21
  111.2 7.3 %collective-permute-start.6 = (f32[3,2048]{1,0:T(4,128)S(1)}, f32[3,2048]{1,0:T(4,128)S(1)}, u32[]{:S(2)}, u32[]{:S(2)}) collective-permute-start(f32[3,2048]{1,0:T(4,128)S(1)} %divide_add_fusion.1), channel_id=1, source_target_pairs={{0,1},{1,2},{2,3},{3,4},{4,5},{5,6},{6,7},{7,8},{8,9},{9,10},{10,1... | collective-permute-start | bytes 73736 | tf_op jit(solution)/shard_map/ppermute | solution.py:10
  115.7 6.1 %collective-permute-start.7 = (f32[3,2048]{1,0:T(4,128)S(1)}, f32[3,2048]{1,0:T(4,128)S(1)}, u32[]{:S(2)}, u32[]{:S(2)}) collective-permute-start(f32[3,2048]{1,0:T(4,128)S(1)} %divide_add_fusion.1), channel_id=1, source_target_pairs={{1,0},{2,1},{3,2},{4,3},{5,4},{6,5},{7,6},{8,7},{9,8},{10,9},{11,1... | collective-permute-start | bytes 73736 | tf_op jit(solution)/shard_map/ppermute | solution.py:10
  143.8 5.0 %collective-permute-start.14 = (f32[3,2048]{1,0:T(4,128)S(1)}, f32[3,2048]{1,0:T(4,128)S(1)}, u32[]{:S(2)}, u32[]{:S(2)}) collective-permute-start(f32[3,2048]{1,0:T(4,128)S(1)} %get-tuple-element.659), channel_id=1, source_target_pairs={{0,1},{1,2},{2,3},{3,4},{4,5},{5,6},{6,7},{7,8},{8,9},{9,10},{10,1... | collective-permute-start | bytes 73736 | tf_op jit(solution)/shard_map/ppermute | solution.py:18
  145.8 6.1 %collective-permute-start.15 = (f32[3,2048]{1,0:T(4,128)S(1)}, f32[3,2048]{1,0:T(4,128)S(1)}, u32[]{:S(2)}, u32[]{:S(2)}) collective-permute-start(f32[3,2048]{1,0:T(4,128)S(1)} %get-tuple-element.660), channel_id=1, source_target_pairs={{1,0},{2,1},{3,2},{4,3},{5,4},{6,5},{7,6},{8,7},{9,8},{10,9},{11,1... | collective-permute-start | bytes 73736 | tf_op jit(solution)/shard_map/ppermute | solution.py:21
where the time goes:
time: 154 us; the launch traced here: 153 us
  starting transfers between devices  44.2 us (29%)
  matrix products  43.9 us (29%)
  other arithmetic  27.4 us (18%)
  local copies, waits for them, and re-layouts  15.1 us (10%)
  waiting for transfers between devices  12.8 us (8%)
  loops' own time  6.94 us (5%)
  between operations  2.32 us (2%)
    ppermute x8, starting transfers between devices, passed_along(): return lax.ppermute(block, axis, route)  23.1 us
    dot_general x65, matrix products, pick_columns(): jnp.einsum('rhl,le->rhe', grid, low_hot, precision=lax.Precision.HIGHEST)  21.5 us
    dot_general x65, matrix products, place_columns(): jnp.einsum('rhe,le->rhl', weighted, low_hot, precision=lax.Precision.HIGH...  21.2 us
    add x64, other arithmetic, place_block(): return (total + place_columns(pieces[0], pieces[1], low, high), None)  18.6 us
    ppermute x4, starting transfers between devices, extended(): lax.ppermute(lax.slice_in_dim(block, block.shape[dim] - width, None, axis...  12.4 us
    ppermute x4, starting transfers between devices, extended(): lax.ppermute(lax.slice_in_dim(block, 0, width, axis=dim), axis, backward)  8.65 us
    ppermute x8, waiting for transfers between devices, passed_along(): return lax.ppermute(block, axis, route)  7.02 us
    ppermute x4, waiting for transfers between devices, extended(): lax.ppermute(lax.slice_in_dim(block, 0, width, axis=dim), axis, backward)  5.81 us
  transfers between devices with their start and end apart: 16, of which 4 were waited for; matrix products, arithmetic and copies ran while one was open for 27% of the time, Pallas kernels for 0%

commit v1 on v0

v1 whole, which is shorter than its diff:
```python
import functools

import jax
import jax.numpy as jnp
from jax import lax
from jax.experimental import pallas as pl
from jax.experimental.pallas import tpu as pltpu
from jax.sharding import PartitionSpec as P

F32 = jnp.float32
BF16 = jnp.bfloat16
I32 = jnp.int32
LANES = 128
OFFSETS = (0, 1, 4, 5)
CHAIN = ("dom", "sub", "lane")


def pieces(x):
    high = x.astype(BF16).astype(F32)
    return high, (x - high).astype(BF16).astype(F32)


def dot(a, b, rhs_dim=0):
    return lax.dot_general(
        a.astype(BF16), b.astype(BF16), (((1,), (rhs_dim,)), ((), ())), preferred_element_type=F32
    )


def iota(shape, dim):
    return lax.broadcasted_iota(I32, shape, dim)


def expanded_matrix(base):
    base_high, base_low = pieces(base)
    row = iota((64, 24), 0)
    comp = row & 3
    pick = jnp.where((iota((64, 24), 1) == comp * 8 + (row >> 3)) & (comp < 3), 1.0, 0.0)
    column = iota((24, 192), 1)
    group = column >> 5
    half = jnp.where(group < 4, group >> 1, group - 4)
    column_comp = column & 3
    node = half * 4 + ((column >> 3) & 3)
    spread = jnp.where((iota((24, 192), 0) == column_comp * 8 + node) & (column_comp < 3), 1.0, 0.0)
    high = dot(dot(pick, base_high), spread)
    low = dot(dot(pick, base_low), spread)
    out_row = iota((64, 192), 0)
    out_column = iota((64, 192), 1)
    same_field = ((out_row >> 2) & 1) == ((out_column >> 2) & 1)
    return jnp.where(same_field, jnp.where(out_column < 128, high, low), 0.0).astype(BF16)


def tiles_of(x):
    return jnp.concatenate(
        [x[:, s : s + LANES] for s in range(0, x.shape[1], LANES)], axis=0
    )


def kernel(
    count,
    disp_ref,
    prev_ref,
    load_ref,
    mass_ref,
    stiff_ref,
    base_ref,
    conn_ref,
    live_ref,
    snode_ref,
    sweight_ref,
    sens_out,
    adj_out,
    resp_out,
    w1,
    w2,
    xs,
    xf,
    p1,
    carry,
    w8,
    send1,
    recv1,
    send2,
    recv2,
):
    nodes = disp_ref.shape[1]
    slots = stiff_ref.shape[1]
    sensors = snode_ref.shape[1]
    n_tiles = nodes // LANES
    own = LANES + nodes
    cells = 2 * nodes + LANES
    lanes_n = lax.axis_size("lane")
    subs_n = lax.axis_size("sub")
    me = (lax.axis_index("dom") * subs_n + lax.axis_index("sub")) * lanes_n + lax.axis_index("lane")

    def there(step):
        other = me + step
        return {
            "dom": lax.div(other, lanes_n * subs_n),
            "sub": lax.rem(lax.div(other, lanes_n), subs_n),
            "lane": lax.rem(other, lanes_n),
        }

    def exists(step):
        return (me + step < count) if step > 0 else (me + step >= 0)

    steps = (1, -1, 2, -2)
    barrier = pltpu.get_barrier_semaphore()
    for step in steps:

        @pl.when(exists(step))
        def _(step=step):
            pl.semaphore_signal(
                barrier, inc=1, device_id=there(step), device_id_type=pl.DeviceIdType.MESH
            )

    sources = {1: (own, nodes), -1: (own, nodes), 2: (own + nodes - LANES, LANES), -2: (own, LANES)}
    targets = {1: LANES, -1: own + nodes, 2: 0, -2: own + 2 * nodes}

    def copy(w, send, recv, which):
        step = steps[which]
        start, width = sources[step]
        return pltpu.make_async_remote_copy(
            src_ref=w.at[:, pl.ds(start, width)],
            dst_ref=w.at[:, pl.ds(targets[step], width)],
            send_sem=send.at[which],
            recv_sem=recv.at[which],
            device_id=there(step),
            device_id_type=pl.DeviceIdType.MESH,
        )

    def start_all(w, send, recv):
        for which, step in enumerate(steps):

            @pl.when(exists(step))
            def _(which=which):
                copy(w, send, recv, which).start()

    def wait_arrivals(w, send, recv):
        for which, step in enumerate(steps):

            @pl.when(exists(-step))
            def _(which=which):
                copy(w, send, recv, which).wait_recv()

    def wait_sent(w, send, recv):
        for which, step in enumerate(steps):

            @pl.when(exists(step))
            def _(which=which):
                copy(w, send, recv, which).wait_send()

    for which, step in enumerate(steps):

        @pl.when(jnp.logical_not(exists(-step)))
        def _(step=step):
            width = sources[step][1]
            zero = jnp.zeros((8, width), F32)
            w1[:, pl.ds(targets[step], width)] = zero
            w2[:, pl.ds(targets[step], width)] = zero

    corner = conn_ref[0:1, :]
    corner_high = corner >> 7
    live = iota((1, slots), 1) < live_ref[0]
    scale_high, scale_low = pieces(jnp.where(live, stiff_ref[...], 0.0))
    rows = iota((8 * n_tiles, slots), 0)
    place = jnp.where((rows & 7) == 3, rows >> 3, jnp.where((rows & 7) == 7, (rows >> 3) + n_tiles, -1))
    on_row = place == corner_high
    weighted = jnp.concatenate(
        [
            jnp.where(on_row, scale_high, 0.0).astype(BF16),
            jnp.where(on_row, scale_low, 0.0).astype(BF16),
        ],
        axis=0,
    )
    low_hot = jnp.where(iota((LANES, slots), 0) == (corner & (LANES - 1)), 1.0, 0.0).astype(BF16)
    both = dot(weighted, low_hot, 1)
    factor = both[: 8 * n_tiles] + both[8 * n_tiles :]

    snode = snode_ref[...]
    sensor_high = snode >> 7
    sensor_hot = jnp.where(iota((LANES, sensors), 0) == (snode & (LANES - 1)), 1.0, 0.0).astype(BF16)
    w8[...] = jnp.zeros((8, sensors), F32)
    w8[4:7, :] = sweight_ref[...]
    weight_high, weight_low = pieces(w8[...])
    stacked = jnp.concatenate(
        [
            jnp.where(sensor_high == h, part, 0.0)
            for part in (weight_high, weight_low)
            for h in range(n_tiles)
        ],
        axis=0,
    )
    placed = dot(stacked, sensor_hot, 1)
    placed = placed[: 8 * n_tiles] + placed[8 * n_tiles :]
    lam2 = jnp.concatenate([placed[8 * h : 8 * h + 8] for h in range(n_tiles)], axis=1)
    factors = jnp.concatenate([factor[8 * h : 8 * h + 8] for h in range(n_tiles)], axis=1)

    inverse = 0.1 / mass_ref[...]
    mu2 = lam2 * inverse
    w1[:, pl.ds(own, nodes)] = mu2 + factors
    disp = disp_ref[...]
    w1[0:3, pl.ds(own, nodes)] = disp

    peers = sum(jnp.where(exists(step), 1, 0) for step in steps)
    pl.semaphore_wait(barrier, peers)

    start_all(w1, send1, recv1)

    lane = iota((8, LANES), 1)

    def shift_tiles(w, first, last, keep):
        def turned(t):
            x = w[:, t * LANES : (t + 1) * LANES]
            return [x] + [pltpu.roll(x, LANES - off, 1) for off in OFFSETS[1:]]

        now = turned(first)
        for t in range(first, last):
            after = turned(t + 1)
            full = jnp.concatenate(
                [now[0]]
                + [
                    jnp.where(lane < LANES - off, now[i], after[i])
                    for i, off in enumerate(OFFSETS)
                    if i > 0
                ],
                axis=0,
            )
            if keep:
                xf[:, t * LANES : (t + 1) * LANES] = full
            high = full.astype(BF16)
            xs[0:32, t * LANES : (t + 1) * LANES] = high
            xs[32:64, t * LANES : (t + 1) * LANES] = (full - high.astype(F32)).astype(BF16)
            now = after

    def operand(start, width):
        return jnp.concatenate(
            [
                xs[:, start : start + width],
                xs[:, start + nodes : start + nodes + width],
                xs[0:32, start : start + width],
                xs[0:32, start + nodes : start + nodes + width],
            ],
            axis=0,
        )

    matrix = expanded_matrix(base_ref[...])
    carry[...] = 2.0 * mu2
    carry[0:3, :] = 2.0 * disp - prev_ref[...] + load_ref[0] * inverse
    first_own = own // LANES
    last_tile = own // LANES + 2 * n_tiles
    shift_tiles(w1, first_own, first_own + n_tiles - 1, False)

    wait_arrivals(w1, send1, recv1)
    shift_tiles(w1, 0, first_own, False)
    shift_tiles(w1, first_own + n_tiles - 1, last_tile, False)

    total = w1[3:4, nodes : nodes + cells] + w1[7:8, 0:cells]
    width = nodes + LANES

    def spread_sum(half0, half1):
        near, far = total[:, nodes:], total[:, :width]
        out = None
        for i, off in enumerate(OFFSETS):
            part = half0[8 * i : 8 * i + 8] * near + half1[8 * i : 8 * i + 8] * far
            part = pltpu.roll(part, off, 1) if off else part
            out = part if out is None else out + part
        return out[:, LANES:]

    p1[...] = dot(matrix, operand(0, cells))
    force = spread_sum(p1[0:32, nodes:], p1[32:64, :width])
    stepped = carry[...] - inverse * force
    w2[:, pl.ds(own, nodes)] = pltpu.roll(stepped, 4, 0)
    start_all(w2, send2, recv2)

    adjoint = pltpu.roll(3.0 * lam2 - 2.0 * force, 4, 0)
    carry[...] = 2.0 * stepped
    carry[0:3, :] = 2.0 * stepped[0:3] - disp + load_ref[1] * inverse

    shift_tiles(w2, first_own, first_own + n_tiles - 1, True)
    wait_arrivals(w2, send2, recv2)
    shift_tiles(w2, 0, first_own, True)
    shift_tiles(w2, first_own + n_tiles - 1, last_tile, True)

    force2 = spread_sum(
        dot(matrix[0:32], operand(nodes, width)), dot(matrix[32:64], operand(0, width))
    )
    adj_out[...] = (adjoint - force2)[0:3]
    final = carry[...] - inverse * pltpu.roll(force2, 4, 0)

    picked = dot(
        jnp.concatenate(pieces(tiles_of(final)), axis=1),
        jnp.concatenate([sensor_hot, sensor_hot], axis=0),
    )
    response = jnp.zeros((8, sensors), F32)
    for h in range(n_tiles):
        response = response + jnp.where(sensor_high == h, picked[8 * h : 8 * h + 8], 0.0)
    resp_out[...] = response[0:3]

    energy = None
    for k in range(8):
        shift = LANES + (k // 4) * nodes
        part = (
            xf[8 * (k % 4) : 8 * (k % 4) + 8, shift : shift + 2 * nodes]
            * p1[8 * k : 8 * k + 8, LANES:cells]
        )
        energy = part if energy is None else energy + part
    table = jnp.concatenate(pieces(tiles_of(energy)), axis=1)
    found = dot(table, jnp.concatenate([low_hot, low_hot], axis=0))
    gathered = jnp.zeros((8, slots), F32)
    for h in range(2 * n_tiles):
        gathered = gathered + jnp.where(corner_high == h, found[8 * h : 8 * h + 8], 0.0)
    gathered = jnp.sum(gathered, axis=0, keepdims=True)
    sens_out[...] = jnp.where(live, -gathered, 0.0)

    wait_sent(w1, send1, recv1)
    wait_sent(w2, send2, recv2)


def per_device(
    displacement,
    previous,
    traffic_load,
    lumped_mass,
    stiffness,
    base_matrix,
    connectivity,
    live_elements,
    sensor_nodes,
    sensor_weights,
):
    nodes = displacement.shape[1]
    slots = connectivity.shape[1]
    sensors = sensor_nodes.shape[0]
    count = lax.axis_size(CHAIN)
    window = 3 * nodes + 2 * LANES
    vmem = pl.BlockSpec(memory_space=pltpu.VMEM)
    smem = pl.BlockSpec(memory_space=pltpu.SMEM)
    sensitivity, adjoint_start, sensor_response = pl.pallas_call(
        functools.partial(kernel, count),
        out_shape=(
            jax.ShapeDtypeStruct((1, slots), F32),
            jax.ShapeDtypeStruct((3, nodes), F32),
            jax.ShapeDtypeStruct((3, sensors), F32),
        ),
        in_specs=[vmem] * 7 + [smem] + [vmem] * 2,
        out_specs=(vmem, vmem, vmem),
        scratch_shapes=[
            pltpu.VMEM((8, window), F32),
            pltpu.VMEM((8, window), F32),
            pltpu.VMEM((64, window), BF16),
            pltpu.VMEM((32, window), F32),
            pltpu.VMEM((64, 2 * nodes + LANES), F32),
            pltpu.VMEM((8, nodes), F32),
            pltpu.VMEM((8, sensors), F32),
            pltpu.SemaphoreType.DMA((4,)),
            pltpu.SemaphoreType.DMA((4,)),
            pltpu.SemaphoreType.DMA((4,)),
            pltpu.SemaphoreType.DMA((4,)),
        ],
        compiler_params=pltpu.CompilerParams(
            collective_id=0, has_side_effects=True, vmem_limit_bytes=32 * 1024 * 1024
        ),
    )(
        displacement,
        previous,
        traffic_load,
        lumped_mass.reshape(1, nodes),
        stiffness.reshape(1, slots),
        base_matrix,
        connectivity,
        live_elements,
        sensor_nodes.reshape(1, sensors),
        sensor_weights,
    )
    return sensitivity.reshape(slots), adjoint_start, sensor_response


def solution(mesh):
    in_specs = (
        P(None, ("event", "dom", "sub", "lane")),
        P(None, ("event", "dom", "sub", "lane")),
        P(None, None, ("event", "dom", "sub", "lane")),
        P(("dom", "sub", "lane")),
        P(("dom", "sub", "lane")),
        P(),
        P(None, ("dom", "sub", "lane")),
        P(("dom", "sub", "lane")),
        P(("dom", "sub", "lane")),
        P(None, ("event", "dom", "sub", "lane")),
    )
    out_specs = (
        P(("event", "dom", "sub", "lane")),
        P(None, ("event", "dom", "sub", "lane")),
        P(None, ("event", "dom", "sub", "lane")),
    )
    return jax.shard_map(
        per_device, mesh=mesh, in_specs=in_specs, out_specs=out_specs, check_vma=False
    )
```

time: 154 us -> 18.1 us (0.12)
  the two profiles are of different devices: /device:TPU:7 before, /device:TPU:0 now
where the time goes in v1:
time: 18.1 us; the launch traced here: 17.8 us
  Pallas kernels  12.3 us (68%)
  local copies, waits for them, and re-layouts  4.13 us (23%)
  between operations  1.43 us (8%)
    pallas_call x1, Pallas kernels, per_device(): pl.pallas_call(functools.partial(kernel, count), out_shape=(jax.ShapeDtyp...  12.3 us
    unnamed x20, local copies, waits for them, and re-layouts  4.13 us

profile of v1, /device:TPU:0, one launch (start us, length us, event | category | flops | bytes accessed | tf_op | source)
XLA Modules:
  0.0 17.8 jit_solution(4064428309139968707)
XLA Ops:
  0.6 0.0 copy-start
  1.3 0.0 copy-start.1
  1.3 0.0 copy-start.3
  1.3 0.0 copy-start.4
  1.4 0.0 copy-start.6
  1.4 0.0 copy-start.7
  1.4 0.9 %copy.13.load_ref = f32[2,3,2048]{2,1,0:T(4,128)S(1)} copy(f32[2,3,2048]{2,0,1:T(2,128)} %param.12) | data formatting | bytes 98304 | tf_op args[2]
  2.2 0.0 copy-done
  2.2 0.0 copy-done.1
  2.3 0.0 copy-done.3
  2.3 0.0 copy-done.4
  2.3 0.0 copy-done.6
  2.3 0.0 copy-done.7
  2.3 0.0 copy-start.2
  2.3 0.7 %copy-done.2 = f32[3,2048]{1,0:T(4,128)S(1)} copy-done((f32[3,2048]{1,0:T(4,128)S(1)}, f32[3,2048]{1,0:T(4,128)}, u32[]{:S(2)}) %copy-start.2) | copy-done | bytes 24600
  3.1 0.0 copy-start.5
  3.1 0.7 %copy-done.5 = f32[2048]{0:T(1024)S(1)} copy-done((f32[2048]{0:T(1024)S(1)}, f32[2048]{0:T(1024)}, u32[]{:S(2)}) %copy-start.5) | copy-done | bytes 8216
  3.8 12.3 %shard_map.121 = (f32[1,2048]{1,0:T(1,128)S(1)}, f32[3,2048]{1,0:T(4,128)S(1)}, f32[3,128]{1,0:T(4,128)S(1)}) custom-call(f32[3,2048]{1,0:T(4,128)S(1)} %copy-done.1, f32[3,2048]{1,0:T(4,128)S(1)} %copy-done.2, f32[2,3,2048]{2,1,0:T(4,128)S(1)} %copy.13.load_ref, f32[1,2048]{1,0:T(1,128)S(1)} %bitcast.4, f32[1,2048]{1,0:T(1,128)S(1)} %bitcast.5, ...), custom_call_target="tpu_custom_call" | custom-call | tf_op jit(solution)/shard_map/pallas_call | solution.py:338
  16.0 0.6 %copy.18 = f32[2048]{0:T(1024)} copy(f32[2048]{0:T(1024)S(1)} %bitcast.6) | data formatting | bytes 16384
  16.6 0.6 %copy.19 = f32[3,2048]{1,0:T(4,128)} copy(f32[3,2048]{1,0:T(4,128)S(1)} %get-tuple-element.13) | data formatting | bytes 49152
  17.2 0.6 %copy.20 = f32[3,128]{1,0:T(4,128)} copy(f32[3,128]{1,0:T(4,128)S(1)} %get-tuple-element.14) | data formatting | bytes 3072
Async XLA Ops:
  0.6 1.6 %copy-start = (s32[8,2048]{1,0:T(8,128)S(1)}, s32[8,2048]{1,0:T(8,128)}, u32[]{:S(2)}) copy-start(s32[8,2048]{1,0:T(8,128)} %conn_ref.1) | copy-start | bytes 196612
  1.3 0.9 %copy-start.1 = (f32[3,2048]{1,0:T(4,128)S(1)}, f32[3,2048]{1,0:T(4,128)}, u32[]{:S(2)}) copy-start(f32[3,2048]{1,0:T(4,128)} %disp_ref.1) | copy-start | bytes 73732
  1.3 0.9 %copy-start.3 = (f32[24,24]{1,0:T(8,128)S(1)}, f32[24,24]{1,0:T(8,128)}, u32[]{:S(2)}) copy-start(f32[24,24]{1,0:T(8,128)} %base_ref.1) | copy-start | bytes 6916
  1.3 0.9 %copy-start.4 = (f32[2048]{0:T(1024)S(1)}, f32[2048]{0:T(1024)}, u32[]{:S(2)}) copy-start(f32[2048]{0:T(1024)} %param.13) | copy-start | bytes 24580
  1.4 0.9 %copy-start.6 = (f32[3,128]{1,0:T(4,128)S(1)}, f32[3,128]{1,0:T(4,128)}, u32[]{:S(2)}) copy-start(f32[3,128]{1,0:T(4,128)} %sweight_ref.1) | copy-start | bytes 4612
  1.4 0.9 %copy-start.7 = (s32[128]{0:T(128)S(1)}, s32[128]{0:T(128)}, u32[]{:S(2)}) copy-start(s32[128]{0:T(128)} %param.18) | copy-start | bytes 1540
  2.3 0.8 %copy-start.2 = (f32[3,2048]{1,0:T(4,128)S(1)}, f32[3,2048]{1,0:T(4,128)}, u32[]{:S(2)}) copy-start(f32[3,2048]{1,0:T(4,128)} %prev_ref.1) | copy-start | bytes 73732
  3.1 0.7 %copy-start.5 = (f32[2048]{0:T(1024)S(1)}, f32[2048]{0:T(1024)}, u32[]{:S(2)}) copy-start(f32[2048]{0:T(1024)} %param.14) | copy-start | bytes 24580

commit v2 on v1

--- a/solution.py
+++ b/solution.py
@@ -55,8 +55,35 @@
     )
 
 
+def row_sums(blocks):
+    sub = iota((8, LANES), 0)
+    step = 4
+    while step:
+        keep = (sub & step) == 0
+        blocks = [
+            jnp.where(keep, a, b)
+            + jnp.where(keep, pltpu.roll(a, 8 - step, 0), pltpu.roll(b, step, 0))
+            for a, b in zip(blocks[:step], blocks[step:])
+        ]
+        step //= 2
+    return blocks[0]
+
+
 def kernel(
     count,
+    disp_hbm,
+    prev_hbm,
+    load_hbm,
+    mass_hbm,
+    stiff_hbm,
+    base_hbm,
+    conn_hbm,
+    live_hbm,
+    snode_hbm,
+    sweight_hbm,
+    sens_out,
+    adj_out,
+    resp_out,
     disp_ref,
     prev_ref,
     load_ref,
@@ -67,11 +94,10 @@
     live_ref,
     snode_ref,
     sweight_ref,
-    sens_out,
-    adj_out,
-    resp_out,
+    loaded,
     w1,
     w2,
+    st,
     xs,
     xf,
     p1,
@@ -81,6 +107,8 @@
     recv1,
     send2,
     recv2,
+    send3,
+    recv3,
 ):
     nodes = disp_ref.shape[1]
     slots = stiff_ref.shape[1]
@@ -112,6 +140,26 @@
             pl.semaphore_signal(
                 barrier, inc=1, device_id=there(step), device_id_type=pl.DeviceIdType.MESH
             )
+
+    loads = {
+        i: pltpu.make_async_copy(source, target, loaded.at[i])
+        for i, (source, target) in enumerate(
+            (
+                (snode_hbm, snode_ref),
+                (sweight_hbm, sweight_ref),
+                (mass_hbm, mass_ref),
+                (disp_hbm, disp_ref),
+                (conn_hbm, conn_ref),
+                (stiff_hbm, stiff_ref),
+                (live_hbm, live_ref),
+                (base_hbm, base_ref),
+                (prev_hbm, prev_ref),
+                (load_hbm, load_ref),
+            )
+        )
+    }
+    for load in loads.values():
+        load.start()
 
     sources = {1: (own, nodes), -1: (own, nodes), 2: (own + nodes - LANES, LANES), -2: (own, LANES)}
     targets = {1: LANES, -1: own + nodes, 2: 0, -2: own + 2 * nodes}
@@ -158,28 +206,28 @@
             w1[:, pl.ds(targets[step], width)] = zero
             w2[:, pl.ds(targets[step], width)] = zero
 
-    corner = conn_ref[0:1, :]
-    corner_high = corner >> 7
-    live = iota((1, slots), 1) < live_ref[0]
-    scale_high, scale_low = pieces(jnp.where(live, stiff_ref[...], 0.0))
-    rows = iota((8 * n_tiles, slots), 0)
-    place = jnp.where((rows & 7) == 3, rows >> 3, jnp.where((rows & 7) == 7, (rows >> 3) + n_tiles, -1))
-    on_row = place == corner_high
-    weighted = jnp.concatenate(
-        [
-            jnp.where(on_row, scale_high, 0.0).astype(BF16),
-            jnp.where(on_row, scale_low, 0.0).astype(BF16),
-        ],
-        axis=0,
-    )
-    low_hot = jnp.where(iota((LANES, slots), 0) == (corner & (LANES - 1)), 1.0, 0.0).astype(BF16)
-    both = dot(weighted, low_hot, 1)
-    factor = both[: 8 * n_tiles] + both[8 * n_tiles :]
-
+    def copy_factors(which):
+        return pltpu.make_async_remote_copy(
+            src_ref=st.at[1],
+            dst_ref=st.at[0 if which == 0 else 2],
+            send_sem=send3.at[which],
+            recv_sem=recv3.at[which],
+            device_id=there(steps[which]),
+            device_id_type=pl.DeviceIdType.MESH,
+        )
+
+    for which in range(2):
+
+        @pl.when(jnp.logical_not(exists(-steps[which])))
+        def _(which=which):
+            st[0 if which == 0 else 2] = jnp.zeros((2 * n_tiles, LANES), F32)
+
+    w8[...] = jnp.zeros((8, sensors), F32)
+    for i in range(4):
+        loads[i].wait()
     snode = snode_ref[...]
     sensor_high = snode >> 7
     sensor_hot = jnp.where(iota((LANES, sensors), 0) == (snode & (LANES - 1)), 1.0, 0.0).astype(BF16)
-    w8[...] = jnp.zeros((8, sensors), F32)
     w8[4:7, :] = sweight_ref[...]
     weight_high, weight_low = pieces(w8[...])
     stacked = jnp.concatenate(
@@ -193,18 +241,42 @@
     placed = dot(stacked, sensor_hot, 1)
     placed = placed[: 8 * n_tiles] + placed[8 * n_tiles :]
     lam2 = jnp.concatenate([placed[8 * h : 8 * h + 8] for h in range(n_tiles)], axis=1)
-    factors = jnp.concatenate([factor[8 * h : 8 * h + 8] for h in range(n_tiles)], axis=1)
 
     inverse = 0.1 / mass_ref[...]
     mu2 = lam2 * inverse
-    w1[:, pl.ds(own, nodes)] = mu2 + factors
+    w1[:, pl.ds(own, nodes)] = mu2
     disp = disp_ref[...]
     w1[0:3, pl.ds(own, nodes)] = disp
 
     peers = sum(jnp.where(exists(step), 1, 0) for step in steps)
     pl.semaphore_wait(barrier, peers)
-
     start_all(w1, send1, recv1)
+
+    for i in range(4, 7):
+        loads[i].wait()
+    corner = conn_ref[0:1, :]
+    corner_high = corner >> 7
+    live = iota((1, slots), 1) < live_ref[0]
+    scale_high, scale_low = pieces(jnp.where(live, stiff_ref[...], 0.0))
+    on_row = iota((2 * n_tiles, slots), 0) == corner_high
+    weighted = jnp.concatenate(
+        [
+            jnp.where(on_row, scale_high, 0.0).astype(BF16),
+            jnp.where(on_row, scale_low, 0.0).astype(BF16),
+        ],
+        axis=0,
+    )
+    low_hot = jnp.where(iota((LANES, slots), 0) == (corner & (LANES - 1)), 1.0, 0.0).astype(BF16)
+    both = dot(weighted, low_hot, 1)
+    st[1] = both[: 2 * n_tiles] + both[2 * n_tiles :]
+    for which in range(2):
+
+        @pl.when(exists(steps[which]))
+        def _(which=which):
+            copy_factors(which).start()
+
+    for i in range(7, 10):
+        loads[i].wait()
 
     lane = iota((8, LANES), 1)
 
@@ -245,7 +317,7 @@
 
     matrix = expanded_matrix(base_ref[...])
     carry[...] = 2.0 * mu2
-    carry[0:3, :] = 2.0 * disp - prev_ref[...] + load_ref[0] * inverse
+    carry[0:3, :] = 2.0 * disp - prev_ref[...] + load_ref[:, 0, :] * inverse
     first_own = own // LANES
     last_tile = own // LANES + 2 * n_tiles
     shift_tiles(w1, first_own, first_own + n_tiles - 1, False)
@@ -254,7 +326,23 @@
     shift_tiles(w1, 0, first_own, False)
     shift_tiles(w1, first_own + n_tiles - 1, last_tile, False)
 
-    total = w1[3:4, nodes : nodes + cells] + w1[7:8, 0:cells]
+    for which in range(2):
+
+        @pl.when(exists(-steps[which]))
+        def _(which=which):
+            copy_factors(which).wait_recv()
+
+    def lower(tile):
+        return st[tile // n_tiles, tile % n_tiles : tile % n_tiles + 1, :]
+
+    def upper(tile):
+        row = n_tiles + tile % n_tiles
+        return st[tile // n_tiles, row : row + 1, :]
+
+    totals = [lower(n_tiles - 1)] + [
+        lower(t + n_tiles) + upper(t) for t in range(2 * n_tiles)
+    ]
+    total = jnp.concatenate([jnp.broadcast_to(x, (8, LANES)) for x in totals], axis=1)
     width = nodes + LANES
 
     def spread_sum(half0, half1):
@@ -274,7 +362,7 @@
 
     adjoint = pltpu.roll(3.0 * lam2 - 2.0 * force, 4, 0)
     carry[...] = 2.0 * stepped
-    carry[0:3, :] = 2.0 * stepped[0:3] - disp + load_ref[1] * inverse
+    carry[0:3, :] = 2.0 * stepped[0:3] - disp + load_ref[:, 1, :] * inverse
 
     shift_tiles(w2, first_own, first_own + n_tiles - 1, True)
     wait_arrivals(w2, send2, recv2)
@@ -304,16 +392,34 @@
             * p1[8 * k : 8 * k + 8, LANES:cells]
         )
         energy = part if energy is None else energy + part
-    table = jnp.concatenate(pieces(tiles_of(energy)), axis=1)
+    tiles = [energy[:, t * LANES : (t + 1) * LANES] for t in range(2 * n_tiles)]
+    sums = jnp.concatenate(
+        [row_sums(tiles[t : t + 8]) for t in range(0, 2 * n_tiles, 8)], axis=0
+    )
+    table = jnp.concatenate(pieces(sums), axis=1)
     found = dot(table, jnp.concatenate([low_hot, low_hot], axis=0))
-    gathered = jnp.zeros((8, slots), F32)
-    for h in range(2 * n_tiles):
-        gathered = gathered + jnp.where(corner_high == h, found[8 * h : 8 * h + 8], 0.0)
-    gathered = jnp.sum(gathered, axis=0, keepdims=True)
+    gathered = jnp.sum(jnp.where(on_row, found, 0.0), axis=0, keepdims=True)
     sens_out[...] = jnp.where(live, -gathered, 0.0)
+
+    for which in range(2):
+
+        @pl.when(exists(steps[which]))
+        def _(which=which):
+            copy_factors(which).wait_send()
 
     wait_sent(w1, send1, recv1)
     wait_sent(w2, send2, recv2)
+
+
+def store_kernel(sens, adj, resp, sens_out, adj_out, resp_out, sem):
+    copies = [
+        pltpu.make_async_copy(source, target, sem.at[i])
+        for i, (source, target) in enumerate(((sens, sens_out), (adj, adj_out), (resp, resp_out)))
+    ]
+    for one in copies:
+        one.start()
+    for one in copies:
+        one.wait()
 
 
 def per_device(
@@ -334,19 +440,36 @@
     count = lax.axis_size(CHAIN)
     window = 3 * nodes + 2 * LANES
     vmem = pl.BlockSpec(memory_space=pltpu.VMEM)
-    smem = pl.BlockSpec(memory_space=pltpu.SMEM)
-    sensitivity, adjoint_start, sensor_response = pl.pallas_call(
+    hbm = pl.BlockSpec(memory_space=pltpu.HBM)
+    operands = (
+        displacement,
+        previous,
+        jnp.transpose(traffic_load, (1, 0, 2)),
+        lumped_mass.reshape(1, nodes),
+        stiffness.reshape(1, slots),
+        base_matrix,
+        connectivity,
+        live_elements,
+        sensor_nodes.reshape(1, sensors),
+        sensor_weights,
+    )
+    results = pl.pallas_call(
         functools.partial(kernel, count),
         out_shape=(
-            jax.ShapeDtypeStruct((1, slots), F32),
-            jax.ShapeDtypeStruct((3, nodes), F32),
-            jax.ShapeDtypeStruct((3, sensors), F32),
+            pltpu.VMEM((1, slots), F32),
+            pltpu.VMEM((3, nodes), F32),
+            pltpu.VMEM((3, sensors), F32),
         ),
-        in_specs=[vmem] * 7 + [smem] + [vmem] * 2,
+        in_specs=[hbm] * len(operands),
         out_specs=(vmem, vmem, vmem),
         scratch_shapes=[
+            (pltpu.SMEM if x is live_elements else pltpu.VMEM)(x.shape, x.dtype) for x in operands
+        ]
+        + [
+            pltpu.SemaphoreType.DMA((len(operands),)),
             pltpu.VMEM((8, window), F32),
             pltpu.VMEM((8, window), F32),
+            pltpu.VMEM((3, 2 * nodes // LANES, LANES), F32),
             pltpu.VMEM((64, window), BF16),
             pltpu.VMEM((32, window), F32),
             pltpu.VMEM((64, 2 * nodes + LANES), F32),
@@ -356,22 +479,20 @@
             pltpu.SemaphoreType.DMA((4,)),
             pltpu.SemaphoreType.DMA((4,)),
             pltpu.SemaphoreType.DMA((4,)),
+            pltpu.SemaphoreType.DMA((2,)),
+            pltpu.SemaphoreType.DMA((2,)),
         ],
         compiler_params=pltpu.CompilerParams(
-            collective_id=0, has_side_effects=True, vmem_limit_bytes=32 * 1024 * 1024
+            collective_id=0, has_side_effects=True, vmem_limit_bytes=60 * 1024 * 1024
         ),
-    )(
-        displacement,
-        previous,
-        traffic_load,
-        lumped_mass.reshape(1, nodes),
-        stiffness.reshape(1, slots),
-        base_matrix,
-        connectivity,
-        live_elements,
-        sensor_nodes.reshape(1, sensors),
-        sensor_weights,
-    )
+    )(*operands)
+    sensitivity, adjoint_start, sensor_response = pl.pallas_call(
+        store_kernel,
+        out_shape=tuple(jax.ShapeDtypeStruct(x.shape, x.dtype) for x in results),
+        in_specs=[vmem] * 3,
+        out_specs=(hbm,) * 3,
+        scratch_shapes=[pltpu.SemaphoreType.DMA((3,))],
+    )(*results)
     return sensitivity.reshape(slots), adjoint_start, sensor_response
 
 

time: 18.1 us -> 17.2 us (0.950)
  local copies, waits for them, and re-layouts: 4.13 us -> 1.79 us
  Pallas kernels: 12.3 us -> 13.9 us
    unnamed x20 -> x6, local copies, waits for them, and re-layouts: 4.13 us -> 1.79 us
    pallas_call x1 -> x2, Pallas kernels: 12.3 us -> 13.9 us  [the longest x1 12.5 us: per_device(): pl.pallas_call(functools.partial(kernel, count), out_shape=(pltpu.VMEM((1...]
where the time goes in v2:
time: 17.2 us; the launch traced here: 17 us
  Pallas kernels  13.9 us (81%)
  local copies, waits for them, and re-layouts  1.79 us (10%)
  between operations  1.3 us (8%)
    pallas_call x1, Pallas kernels, per_device(): pl.pallas_call(functools.partial(kernel, count), out_shape=(pltpu.VMEM((1...  12.5 us
    unnamed x6, local copies, waits for them, and re-layouts  1.79 us
    pallas_call x1, Pallas kernels, per_device(): pl.pallas_call(store_kernel, out_shape=tuple((jax.ShapeDtypeStruct(x.shap...  1.4 us

profile of v2, /device:TPU:0, one launch (start us, length us, event | category | flops | bytes accessed | tf_op | source)
XLA Modules:
  0.0 17.0 jit_solution(1252854306594056782)
XLA Ops:
  1.3 12.5 %shard_map.121 = (f32[1,2048]{1,0:T(1,128)S(1)}, f32[3,2048]{1,0:T(4,128)S(1)}, f32[3,128]{1,0:T(4,128)S(1)}) custom-call(f32[3,2048]{1,0:T(4,128)} %disp_hbm.1, f32[3,2048]{1,0:T(4,128)} %prev_hbm.1, f32[3,2,2048]{2,1,0:T(2,128)} %bitcast.5, f32[1,2048]{1,0:T(1,128)} %bitcast.6, f32[1,2048]{1,0:T(1,128)} %bitcast.7, f32[24,24]{1,0:T(8,128)} %base_hbm.1, ...), custom_call_target="tpu_custom_call" | custom-call | tf_op jit(solution)/shard_map/pallas_call | solution.py:456
  13.8 0.0 copy-start
  13.8 0.6 %copy-done = f32[3,2048]{1,0:T(4,128)} copy-done((f32[3,2048]{1,0:T(4,128)}, f32[3,2048]{1,0:T(4,128)S(1)}, u32[]{:S(2)}) %copy-start) | copy-done | bytes 24600
  14.4 0.0 copy-start.1
  14.4 0.6 %copy-done.1 = f32[1,2048]{1,0:T(1,128)} copy-done((f32[1,2048]{1,0:T(1,128)}, f32[1,2048]{1,0:T(1,128)S(1)}, u32[]{:S(2)}) %copy-start.1) | copy-done | bytes 8216
  15.0 0.0 copy-start.2
  15.0 0.6 %copy-done.2 = f32[3,128]{1,0:T(4,128)} copy-done((f32[3,128]{1,0:T(4,128)}, f32[3,128]{1,0:T(4,128)S(1)}, u32[]{:S(2)}) %copy-start.2) | copy-done | bytes 1560
  15.6 1.4 %shard_map.122 = (f32[1,2048]{1,0:T(1,128)}, f32[3,2048]{1,0:T(4,128)}, f32[3,128]{1,0:T(4,128)}) custom-call(f32[1,2048]{1,0:T(1,128)} %copy-done.1, f32[3,2048]{1,0:T(4,128)} %copy-done, f32[3,128]{1,0:T(4,128)} %copy-done.2), custom_call_target="tpu_custom_call" | custom-call | tf_op jit(solution)/shard_map/pallas_call | solution.py:489
Async XLA Ops:
  13.8 0.6 %copy-start = (f32[3,2048]{1,0:T(4,128)}, f32[3,2048]{1,0:T(4,128)S(1)}, u32[]{:S(2)}) copy-start(f32[3,2048]{1,0:T(4,128)S(1)} %get-tuple-element.10.adj) | copy-start | bytes 73732
  14.4 0.6 %copy-start.1 = (f32[1,2048]{1,0:T(1,128)}, f32[1,2048]{1,0:T(1,128)S(1)}, u32[]{:S(2)}) copy-start(f32[1,2048]{1,0:T(1,128)S(1)} %get-tuple-element.9.sens) | copy-start | bytes 24580
  15.0 0.6 %copy-start.2 = (f32[3,128]{1,0:T(4,128)}, f32[3,128]{1,0:T(4,128)S(1)}, u32[]{:S(2)}) copy-start(f32[3,128]{1,0:T(4,128)S(1)} %get-tuple-element.11.resp) | copy-start | bytes 4612

commit v3 on v2

--- a/solution.py
+++ b/solution.py
@@ -492,6 +492,7 @@
         in_specs=[vmem] * 3,
         out_specs=(hbm,) * 3,
         scratch_shapes=[pltpu.SemaphoreType.DMA((3,))],
+        compiler_params=pltpu.CompilerParams(vmem_limit_bytes=4 * 1024 * 1024),
     )(*results)
     return sensitivity.reshape(slots), adjoint_start, sensor_response
 

time: 17.2 us -> 14.6 us (0.85)
  local copies, waits for them, and re-layouts: 1.79 us -> 0 us
  Pallas kernels: 13.9 us -> 13.1 us
    unnamed x6 -> x0, local copies, waits for them, and re-layouts: 1.79 us -> none
    pallas_call x1, Pallas kernels: 1.4 us -> 0.65 us  [per_device(): pl.pallas_call(store_kernel, out_shape=tuple((jax.ShapeDtypeStruct(x.shap...]
where the time goes in v3:
time: 14.6 us; the launch traced here: 14.4 us
  Pallas kernels  13.1 us (90%)
  between operations  1.29 us (9%)
    pallas_call x1, Pallas kernels, per_device(): pl.pallas_call(functools.partial(kernel, count), out_shape=(pltpu.VMEM((1...  12.5 us
    pallas_call x1, Pallas kernels, per_device(): pl.pallas_call(store_kernel, out_shape=tuple((jax.ShapeDtypeStruct(x.shap...  0.65 us

profile of v3, /device:TPU:0, one launch (start us, length us, event | category | flops | bytes accessed | tf_op | source)
XLA Modules:
  0.0 14.4 jit_solution(684072426215924644)
XLA Ops:
  1.3 12.5 %shard_map.121 = (f32[1,2048]{1,0:T(1,128)S(1)}, f32[3,2048]{1,0:T(4,128)S(1)}, f32[3,128]{1,0:T(4,128)S(1)}) custom-call(f32[3,2048]{1,0:T(4,128)} %disp_hbm.1, f32[3,2048]{1,0:T(4,128)} %prev_hbm.1, f32[3,2,2048]{2,1,0:T(2,128)} %bitcast.5, f32[1,2048]{1,0:T(1,128)} %bitcast.6, f32[1,2048]{1,0:T(1,128)} %bitcast.7, f32[24,24]{1,0:T(8,128)} %base_hbm.1, ...), custom_call_target="tpu_custom_call" | custom-call | tf_op jit(solution)/shard_map/pallas_call | solution.py:456
  13.8 0.6 %shard_map.122 = (f32[1,2048]{1,0:T(1,128)}, f32[3,2048]{1,0:T(4,128)}, f32[3,128]{1,0:T(4,128)}) custom-call(f32[1,2048]{1,0:T(1,128)S(1)} %get-tuple-element.9.sens, f32[3,2048]{1,0:T(4,128)S(1)} %get-tuple-element.10.adj, f32[3,128]{1,0:T(4,128)S(1)} %get-tuple-element.11.resp), custom_call_target="tpu_custom_call" | custom-call | tf_op jit(solution)/shard_map/pallas_call | solution.py:489

commit v4 on v3

--- a/solution.py
+++ b/solution.py
@@ -164,38 +164,62 @@
     sources = {1: (own, nodes), -1: (own, nodes), 2: (own + nodes - LANES, LANES), -2: (own, LANES)}
     targets = {1: LANES, -1: own + nodes, 2: 0, -2: own + 2 * nodes}
 
-    def copy(w, send, recv, which):
-        step = steps[which]
-        start, width = sources[step]
+    mid = n_tiles // 2
+    own_tile = 1 + n_tiles
+    first_tile = {1: 1, -1: 1 + 2 * n_tiles, 2: 1 - n_tiles, -2: 1 + 3 * n_tiles}
+    parts1 = (
+        (1, 0, mid + 2),
+        (-1, 0, mid + 2),
+        (1, mid + 2, n_tiles - mid - 2),
+        (-1, mid + 2, n_tiles - mid - 2),
+        (2, n_tiles - 1, 1),
+        (-2, 0, 1),
+    )
+    parts2 = (
+        (1, 1, mid),
+        (-1, 1, mid),
+        (1, mid + 1, n_tiles - mid - 1),
+        (-1, mid + 1, n_tiles - mid - 1),
+        (1, 0, 1),
+        (-1, 0, 1),
+        (2, n_tiles - 1, 1),
+        (-2, 0, 1),
+    )
+    exchange1 = (w1, send1, recv1, parts1)
+    exchange2 = (w2, send2, recv2, parts2)
+
+    def copy(exchange, which):
+        w, send, recv, parts = exchange
+        step, first, tiles = parts[which]
         return pltpu.make_async_remote_copy(
-            src_ref=w.at[:, pl.ds(start, width)],
-            dst_ref=w.at[:, pl.ds(targets[step], width)],
+            src_ref=w.at[:, pl.ds((own_tile + first) * LANES, tiles * LANES)],
+            dst_ref=w.at[:, pl.ds((first_tile[step] + first) * LANES, tiles * LANES)],
             send_sem=send.at[which],
             recv_sem=recv.at[which],
             device_id=there(step),
             device_id_type=pl.DeviceIdType.MESH,
         )
 
-    def start_all(w, send, recv):
-        for which, step in enumerate(steps):
-
-            @pl.when(exists(step))
+    def start(exchange, first, last):
+        for which in range(first, last):
+
+            @pl.when(exists(exchange[3][which][0]))
             def _(which=which):
-                copy(w, send, recv, which).start()
-
-    def wait_arrivals(w, send, recv):
-        for which, step in enumerate(steps):
-
-            @pl.when(exists(-step))
+                copy(exchange, which).start()
+
+    def wait_arrivals(exchange, first, last):
+        for which in range(first, last):
+
+            @pl.when(exists(-exchange[3][which][0]))
             def _(which=which):
-                copy(w, send, recv, which).wait_recv()
-
-    def wait_sent(w, send, recv):
-        for which, step in enumerate(steps):
-
-            @pl.when(exists(step))
+                copy(exchange, which).wait_recv()
+
+    def wait_sent(exchange):
+        for which in range(len(exchange[3])):
+
+            @pl.when(exists(exchange[3][which][0]))
             def _(which=which):
-                copy(w, send, recv, which).wait_send()
+                copy(exchange, which).wait_send()
 
     for which, step in enumerate(steps):
 
@@ -250,7 +274,7 @@
 
     peers = sum(jnp.where(exists(step), 1, 0) for step in steps)
     pl.semaphore_wait(barrier, peers)
-    start_all(w1, send1, recv1)
+    start(exchange1, 0, 6)
 
     for i in range(4, 7):
         loads[i].wait()
@@ -318,13 +342,11 @@
     matrix = expanded_matrix(base_ref[...])
     carry[...] = 2.0 * mu2
     carry[0:3, :] = 2.0 * disp - prev_ref[...] + load_ref[:, 0, :] * inverse
-    first_own = own // LANES
-    last_tile = own // LANES + 2 * n_tiles
-    shift_tiles(w1, first_own, first_own + n_tiles - 1, False)
-
-    wait_arrivals(w1, send1, recv1)
-    shift_tiles(w1, 0, first_own, False)
-    shift_tiles(w1, first_own + n_tiles - 1, last_tile, False)
+    last_tile = own_tile + 2 * n_tiles
+    shift_tiles(w1, own_tile, own_tile + n_tiles - 1, False)
+    wait_arrivals(exchange1, 0, 2)
+    shift_tiles(w1, 1, mid + 2, False)
+    shift_tiles(w1, own_tile + n_tiles, own_tile + n_tiles + mid + 1, False)
 
     for which in range(2):
 
@@ -342,11 +364,11 @@
     totals = [lower(n_tiles - 1)] + [
         lower(t + n_tiles) + upper(t) for t in range(2 * n_tiles)
     ]
-    total = jnp.concatenate([jnp.broadcast_to(x, (8, LANES)) for x in totals], axis=1)
-    width = nodes + LANES
-
-    def spread_sum(half0, half1):
-        near, far = total[:, nodes:], total[:, :width]
+    totals = [jnp.broadcast_to(x, (8, LANES)) for x in totals]
+
+    def spread_sum(first, last, half0, half1):
+        near = jnp.concatenate(totals[first + n_tiles : last + n_tiles + 1], axis=1)
+        far = jnp.concatenate(totals[first : last + 1], axis=1)
         out = None
         for i, off in enumerate(OFFSETS):
             part = half0[8 * i : 8 * i + 8] * near + half1[8 * i : 8 * i + 8] * far
@@ -354,23 +376,59 @@
             out = part if out is None else out + part
         return out[:, LANES:]
 
-    p1[...] = dot(matrix, operand(0, cells))
-    force = spread_sum(p1[0:32, nodes:], p1[32:64, :width])
-    stepped = carry[...] - inverse * force
-    w2[:, pl.ds(own, nodes)] = pltpu.roll(stepped, 4, 0)
-    start_all(w2, send2, recv2)
+    def multiply(first, last):
+        p1[:, first * LANES : last * LANES] = dot(
+            matrix, operand(first * LANES, (last - first) * LANES)
+        )
+
+    def step_one(first, last):
+        force = spread_sum(
+            first,
+            last,
+            p1[0:32, (first + n_tiles) * LANES : (last + n_tiles + 1) * LANES],
+            p1[32:64, first * LANES : (last + 1) * LANES],
+        )
+        here = slice(first * LANES, last * LANES)
+        stepped = carry[:, here] - inverse[:, here] * force
+        w2[:, (own_tile + first) * LANES : (own_tile + last) * LANES] = pltpu.roll(stepped, 4, 0)
+        return force, stepped
+
+    multiply(1, mid + 2)
+    multiply(own_tile, own_tile + mid + 1)
+    force_a, stepped_a = step_one(1, mid + 1)
+    start(exchange2, 0, 2)
+
+    wait_arrivals(exchange1, 2, 6)
+    shift_tiles(w1, 0, 1, False)
+    shift_tiles(w1, mid + 2, own_tile, False)
+    shift_tiles(w1, own_tile + n_tiles - 1, own_tile + n_tiles, False)
+    shift_tiles(w1, own_tile + n_tiles + mid + 1, last_tile, False)
+    multiply(0, 1)
+    multiply(mid + 2, own_tile)
+    multiply(own_tile + mid + 1, 1 + 2 * n_tiles)
+    force_0, stepped_0 = step_one(0, 1)
+    force_b, stepped_b = step_one(mid + 1, n_tiles)
+    start(exchange2, 2, 8)
+    force = jnp.concatenate([force_0, force_a, force_b], axis=1)
+    stepped = jnp.concatenate([stepped_0, stepped_a, stepped_b], axis=1)
 
     adjoint = pltpu.roll(3.0 * lam2 - 2.0 * force, 4, 0)
     carry[...] = 2.0 * stepped
     carry[0:3, :] = 2.0 * stepped[0:3] - disp + load_ref[:, 1, :] * inverse
 
-    shift_tiles(w2, first_own, first_own + n_tiles - 1, True)
-    wait_arrivals(w2, send2, recv2)
-    shift_tiles(w2, 0, first_own, True)
-    shift_tiles(w2, first_own + n_tiles - 1, last_tile, True)
-
+    shift_tiles(w2, own_tile, own_tile + n_tiles - 1, True)
+    wait_arrivals(exchange2, 0, 2)
+    shift_tiles(w2, 2, mid + 1, True)
+    shift_tiles(w2, own_tile + n_tiles + 1, own_tile + n_tiles + mid, True)
+    wait_arrivals(exchange2, 2, 8)
+    shift_tiles(w2, 0, 2, True)
+    shift_tiles(w2, mid + 1, own_tile, True)
+    shift_tiles(w2, own_tile + n_tiles - 1, own_tile + n_tiles + 1, True)
+    shift_tiles(w2, own_tile + n_tiles + mid, last_tile, True)
+
+    width = nodes + LANES
     force2 = spread_sum(
-        dot(matrix[0:32], operand(nodes, width)), dot(matrix[32:64], operand(0, width))
+        0, n_tiles, dot(matrix[0:32], operand(nodes, width)), dot(matrix[32:64], operand(0, width))
     )
     adj_out[...] = (adjoint - force2)[0:3]
     final = carry[...] - inverse * pltpu.roll(force2, 4, 0)
@@ -407,8 +465,8 @@
         def _(which=which):
             copy_factors(which).wait_send()
 
-    wait_sent(w1, send1, recv1)
-    wait_sent(w2, send2, recv2)
+    wait_sent(exchange1)
+    wait_sent(exchange2)
 
 
 def store_kernel(sens, adj, resp, sens_out, adj_out, resp_out, sem):
@@ -475,10 +533,10 @@
             pltpu.VMEM((64, 2 * nodes + LANES), F32),
             pltpu.VMEM((8, nodes), F32),
             pltpu.VMEM((8, sensors), F32),
-            pltpu.SemaphoreType.DMA((4,)),
-            pltpu.SemaphoreType.DMA((4,)),
-            pltpu.SemaphoreType.DMA((4,)),
-            pltpu.SemaphoreType.DMA((4,)),
+            pltpu.SemaphoreType.DMA((6,)),
+            pltpu.SemaphoreType.DMA((6,)),
+            pltpu.SemaphoreType.DMA((8,)),
+            pltpu.SemaphoreType.DMA((8,)),
             pltpu.SemaphoreType.DMA((2,)),
             pltpu.SemaphoreType.DMA((2,)),
         ],

time: 14.6 us -> 14 us (0.959)
  Pallas kernels: 13.1 us -> 12.5 us
    pallas_call x1, Pallas kernels: 12.5 us -> 11.9 us  [per_device(): pl.pallas_call(functools.partial(kernel, count), out_shape=(pltpu.VMEM((1...]
where the time goes in v4:
time: 14 us; the launch traced here: 13.8 us
  Pallas kernels  12.5 us (89%)
  between operations  1.29 us (9%)
    pallas_call x1, Pallas kernels, per_device(): pl.pallas_call(functools.partial(kernel, count), out_shape=(pltpu.VMEM((1...  11.9 us
    pallas_call x1, Pallas kernels, per_device(): pl.pallas_call(store_kernel, out_shape=tuple((jax.ShapeDtypeStruct(x.shap...  0.65 us

profile of v4, /device:TPU:0, one launch (start us, length us, event | category | flops | bytes accessed | tf_op | source)
XLA Modules:
  0.0 13.8 jit_solution(14905081623217666799)
XLA Ops:
  1.3 11.9 %shard_map.121 = (f32[1,2048]{1,0:T(1,128)S(1)}, f32[3,2048]{1,0:T(4,128)S(1)}, f32[3,128]{1,0:T(4,128)S(1)}) custom-call(f32[3,2048]{1,0:T(4,128)} %disp_hbm.1, f32[3,2048]{1,0:T(4,128)} %prev_hbm.1, f32[3,2,2048]{2,1,0:T(2,128)} %bitcast.5, f32[1,2048]{1,0:T(1,128)} %bitcast.6, f32[1,2048]{1,0:T(1,128)} %bitcast.7, f32[24,24]{1,0:T(8,128)} %base_hbm.1, ...), custom_call_target="tpu_custom_call" | custom-call | tf_op jit(solution)/shard_map/pallas_call | solution.py:514
  13.2 0.6 %shard_map.122 = (f32[1,2048]{1,0:T(1,128)}, f32[3,2048]{1,0:T(4,128)}, f32[3,128]{1,0:T(4,128)}) custom-call(f32[1,2048]{1,0:T(1,128)S(1)} %get-tuple-element.9.sens, f32[3,2048]{1,0:T(4,128)S(1)} %get-tuple-element.10.adj, f32[3,128]{1,0:T(4,128)S(1)} %get-tuple-element.11.resp), custom_call_target="tpu_custom_call" | custom-call | tf_op jit(solution)/shard_map/pallas_call | solution.py:547

commit v5 on v4

--- a/solution.py
+++ b/solution.py
@@ -101,6 +101,7 @@
     xs,
     xf,
     p1,
+    p2,
     carry,
     w8,
     send1,
@@ -416,20 +417,41 @@
     carry[...] = 2.0 * stepped
     carry[0:3, :] = 2.0 * stepped[0:3] - disp + load_ref[:, 1, :] * inverse
 
+    def multiply_two(first, last):
+        width = (last - first) * LANES
+        here = slice(first * LANES, last * LANES)
+        p2[0:32, here] = dot(matrix[0:32], operand(first * LANES + nodes, width))
+        p2[32:64, here] = dot(matrix[32:64], operand(first * LANES, width))
+
+    def energy_of(first, last):
+        found = {}
+        for t in range(first, last):
+            value = None
+            for k in range(8):
+                at = (t + (k // 4) * n_tiles) * LANES
+                part = (
+                    xf[8 * (k % 4) : 8 * (k % 4) + 8, at : at + LANES]
+                    * p1[8 * k : 8 * k + 8, t * LANES : (t + 1) * LANES]
+                )
+                value = part if value is None else value + part
+            found[t] = value
+        return found
+
     shift_tiles(w2, own_tile, own_tile + n_tiles - 1, True)
     wait_arrivals(exchange2, 0, 2)
     shift_tiles(w2, 2, mid + 1, True)
     shift_tiles(w2, own_tile + n_tiles + 1, own_tile + n_tiles + mid, True)
+    multiply_two(2, mid + 1)
+    energy = energy_of(2, mid + 1) | energy_of(own_tile + 1, own_tile + mid)
     wait_arrivals(exchange2, 2, 8)
     shift_tiles(w2, 0, 2, True)
     shift_tiles(w2, mid + 1, own_tile, True)
     shift_tiles(w2, own_tile + n_tiles - 1, own_tile + n_tiles + 1, True)
     shift_tiles(w2, own_tile + n_tiles + mid, last_tile, True)
 
-    width = nodes + LANES
-    force2 = spread_sum(
-        0, n_tiles, dot(matrix[0:32], operand(nodes, width)), dot(matrix[32:64], operand(0, width))
-    )
+    multiply_two(0, 2)
+    multiply_two(mid + 1, n_tiles + 1)
+    force2 = spread_sum(0, n_tiles, p2[0:32, :], p2[32:64, :])
     adj_out[...] = (adjoint - force2)[0:3]
     final = carry[...] - inverse * pltpu.roll(force2, 4, 0)
 
@@ -442,15 +464,9 @@
         response = response + jnp.where(sensor_high == h, picked[8 * h : 8 * h + 8], 0.0)
     resp_out[...] = response[0:3]
 
-    energy = None
-    for k in range(8):
-        shift = LANES + (k // 4) * nodes
-        part = (
-            xf[8 * (k % 4) : 8 * (k % 4) + 8, shift : shift + 2 * nodes]
-            * p1[8 * k : 8 * k + 8, LANES:cells]
-        )
-        energy = part if energy is None else energy + part
-    tiles = [energy[:, t * LANES : (t + 1) * LANES] for t in range(2 * n_tiles)]
+    energy |= energy_of(1, 2) | energy_of(mid + 1, own_tile + 1)
+    energy |= energy_of(own_tile + mid, own_tile + n_tiles)
+    tiles = [energy[t + 1] for t in range(2 * n_tiles)]
     sums = jnp.concatenate(
         [row_sums(tiles[t : t + 8]) for t in range(0, 2 * n_tiles, 8)], axis=0
     )
@@ -531,6 +547,7 @@
             pltpu.VMEM((64, window), BF16),
             pltpu.VMEM((32, window), F32),
             pltpu.VMEM((64, 2 * nodes + LANES), F32),
+            pltpu.VMEM((64, nodes + LANES), F32),
             pltpu.VMEM((8, nodes), F32),
             pltpu.VMEM((8, sensors), F32),
             pltpu.SemaphoreType.DMA((6,)),

time: 14 us -> 14 us (level)
  no operation moved by 1% of the time
where the time goes in v5:
time: 14 us; the launch traced here: 13.8 us
  Pallas kernels  12.5 us (89%)
  between operations  1.29 us (9%)
    pallas_call x1, Pallas kernels, per_device(): pl.pallas_call(functools.partial(kernel, count), out_shape=(pltpu.VMEM((1...  11.8 us
    pallas_call x1, Pallas kernels, per_device(): pl.pallas_call(store_kernel, out_shape=tuple((jax.ShapeDtypeStruct(x.shap...  0.65 us

profile of v5, /device:TPU:0, one launch (start us, length us, event | category | flops | bytes accessed | tf_op | source)
XLA Modules:
  0.0 13.8 jit_solution(2661012454780764442)
XLA Ops:
  1.3 11.8 %shard_map.121 = (f32[1,2048]{1,0:T(1,128)S(1)}, f32[3,2048]{1,0:T(4,128)S(1)}, f32[3,128]{1,0:T(4,128)S(1)}) custom-call(f32[3,2048]{1,0:T(4,128)} %disp_hbm.1, f32[3,2048]{1,0:T(4,128)} %prev_hbm.1, f32[3,2,2048]{2,1,0:T(2,128)} %bitcast.5, f32[1,2048]{1,0:T(1,128)} %bitcast.6, f32[1,2048]{1,0:T(1,128)} %bitcast.7, f32[24,24]{1,0:T(8,128)} %base_hbm.1, ...), custom_call_target="tpu_custom_call" | custom-call | tf_op jit(solution)/shard_map/pallas_call | solution.py:530
  13.1 0.6 %shard_map.122 = (f32[1,2048]{1,0:T(1,128)}, f32[3,2048]{1,0:T(4,128)}, f32[3,128]{1,0:T(4,128)}) custom-call(f32[1,2048]{1,0:T(1,128)S(1)} %get-tuple-element.9.sens, f32[3,2048]{1,0:T(4,128)S(1)} %get-tuple-element.10.adj, f32[3,128]{1,0:T(4,128)S(1)} %get-tuple-element.11.resp), custom_call_target="tpu_custom_call" | custom-call | tf_op jit(solution)/shard_map/pallas_call | solution.py:564
